TPU v7x, 512 devices: a whole 4x8x8 slice. The times are simulated.
512 devices in a mesh: col: 64 (over y, z_lo, core), row: 8 (over x, z_hi).
Axes of the slice: x: 4, y: 8, z: 8 (z_hi: 2, z_lo: 4; z = z_hi * 4 + z_lo), core: 2. Of those that a mesh axis runs over, the one named last changes fastest.
Arguments:
- field: bfloat16 [128, 1024, 128], P('row', 'col'), may hold values from -6 to 6
- cotangent: bfloat16 [128, 1024, 128], P('row', 'col'), may hold values from -6 to 6
- w_first: bfloat16 [3, 3, 128, 128], replicated, may hold values from -0.1875 to 0.1875
- w_down: bfloat16 [3, 3, 128, 256], replicated, may hold values from -0.1875 to 0.1875
- w_up: bfloat16 [2, 2, 256, 128], replicated, may hold values from -0.375 to 0.375
- offsets: int32 [8, 64, 2], replicated, may hold values from -8 to 8
- blend_table: int32 [32, 32], replicated, may hold values from 1 to 16
Outputs:
- blended: bfloat16 [128, 1024, 128], P('row', 'col')
- field_grad: float32 [128, 1024, 128], P('row', 'col')
- grad_first: float32 [3, 3, 128, 128], replicated
- grad_down: float32 [3, 3, 128, 256], replicated
- grad_up: float32 [2, 2, 256, 128], replicated
Inputs may be any that keep to these rules, and one draw needn't show every extreme that they name: `offsets`: A patch's first cell lies 8 cells minus its offset before its tile's first cell on each axis.
All inputs are finite; a program needn't handle non-finite values.
Results may differ from a plain program's by a relative error of at most 0.015.
Values may be sent and summed in bfloat16 or wider, within the bound.
No kernel may reach another device: no remote copies, remote signals or barrier semaphores. Data moves between devices by JAX's collectives and lax.ppermute only.
A program may use at most 64 MiB of HBM per device.

v0:
```python
import math
import jax
import jax.numpy as jnp
from jax import lax
from jax.sharding import PartitionSpec as P

MARGIN = 8


def passed_along(block, axis, distance):
    devices = range(lax.axis_size(axis))
    route = [(i - distance, i) for i in devices if i - distance in devices]
    return lax.ppermute(block, axis, route)


def extended(x, sides, width):
    for axis, dim in sides:
        size, length = (lax.axis_size(axis), x.shape[dim])
        up = [(i, (i + 1) % size) for i in range(size - 1)]
        down = [(j, i) for i, j in up]
        last = lax.slice_in_dim(x, length - width, length, axis=dim)
        leading = lax.slice_in_dim(x, 0, width, axis=dim)
        before = lax.ppermute(last, axis, up)
        after = lax.ppermute(leading, axis, down)
        x = jnp.concatenate([before, x, after], axis=dim)
    return x


def conv_same(inputs, kernel):
    rows, cols, chans = inputs.shape
    padded = jnp.pad(inputs, ((1, 1), (1, 1), (0, 0)))
    total = jnp.zeros((rows * cols, kernel.shape[3]), jnp.float32)
    for row_tap in range(3):
        for col_tap in range(3):
            window = padded[row_tap : row_tap + rows, col_tap : col_tap + cols].reshape(
                rows * cols, chans
            )
            total = total + jnp.dot(
                window, kernel[row_tap, col_tap], preferred_element_type=jnp.float32
            )
    return total.reshape(rows, cols, kernel.shape[3])


def conv_down(inputs, kernel):
    rows, cols, chans = inputs.shape
    padded = jnp.pad(inputs, ((1, 1), (1, 1), (0, 0)))
    half_r = rows // 2
    half_c = cols // 2
    total = jnp.zeros((half_r * half_c, kernel.shape[3]), jnp.float32)
    for row_tap in range(3):
        for col_tap in range(3):
            window = padded[row_tap : row_tap + rows : 2, col_tap : col_tap + cols : 2].reshape(
                half_r * half_c, chans
            )
            total = total + jnp.dot(
                window, kernel[row_tap, col_tap], preferred_element_type=jnp.float32
            )
    return total.reshape(half_r, half_c, kernel.shape[3])


def conv_up(inputs, kernel):
    rows, cols, chans = inputs.shape
    flat = inputs.reshape(rows * cols, chans)
    lines = []
    for row_tap in range(2):
        pieces = []
        for col_tap in range(2):
            pieces.append(
                jnp.dot(flat, kernel[row_tap, col_tap], preferred_element_type=jnp.float32).reshape(
                    rows, cols, kernel.shape[3]
                )
            )
        lines.append(jnp.stack(pieces, axis=2))
    return jnp.stack(lines, axis=1).reshape(2 * rows, 2 * cols, kernel.shape[3])


def patch_net(patch, w_first, w_down, w_up):
    hidden = jax.nn.silu(conv_same(patch, w_first)).astype(jnp.bfloat16)
    lower = jax.nn.silu(conv_down(hidden, w_down)).astype(jnp.bfloat16)
    return hidden.astype(jnp.float32) + conv_up(lower, w_up)


def return_margins(canvas, tile_h, tile_w, edge):
    summed = canvas
    for heading in (1, -1):
        strip = canvas[tile_h + edge :] if heading == 1 else canvas[:edge]
        arrived = passed_along(strip.astype(jnp.bfloat16), "row", heading).astype(strip.dtype)
        if heading == 1:
            summed = summed.at[edge : 2 * edge].add(arrived)
        else:
            summed = summed.at[tile_h : tile_h + edge].add(arrived)
    middle = summed[edge : tile_h + edge]
    result = middle
    for heading in (1, -1):
        strip = middle[:, tile_w + edge :] if heading == 1 else middle[:, :edge]
        arrived = passed_along(strip.astype(jnp.bfloat16), "col", heading).astype(strip.dtype)
        if heading == 1:
            result = result.at[:, edge : 2 * edge].add(arrived)
        else:
            result = result.at[:, tile_w : tile_w + edge].add(arrived)
    return result[:, edge : tile_w + edge]


def weight_total(offsets, table_f, row_at, col_at, rows_n, cols_n, tile_h, tile_w, lead, reach):
    patch_h, patch_w = table_f.shape
    total = jnp.zeros((tile_h + 2 * lead, tile_w + 2 * lead), jnp.float32)
    for row_step in range(-reach, reach + 1):
        for col_step in range(-reach, reach + 1):
            near_row = row_at + row_step
            near_col = col_at + col_step
            inside = (
                (near_row >= 0) & (near_row < rows_n) & (near_col >= 0) & (near_col < cols_n)
            ).astype(jnp.float32)
            shift_pair = offsets[
                jnp.clip(near_row, 0, rows_n - 1), jnp.clip(near_col, 0, cols_n - 1)
            ]
            top = row_step * tile_h - MARGIN + shift_pair[0] + lead
            left = col_step * tile_w - MARGIN + shift_pair[1] + lead
            pick_rows = (
                jnp.arange(tile_h + 2 * lead)[:, None] - top == jnp.arange(patch_h)[None, :]
            ).astype(jnp.float32)
            pick_cols = (
                jnp.arange(tile_w + 2 * lead)[:, None] - left == jnp.arange(patch_w)[None, :]
            ).astype(jnp.float32)
            placed = jnp.dot(
                jnp.dot(pick_rows, table_f, precision=lax.Precision.HIGHEST),
                pick_cols.T,
                precision=lax.Precision.HIGHEST,
            )
            total = total + inside * placed
    return total


def per_device(field, cotangent, w_first, w_down, w_up, offsets, blend_table):
    tile_h, tile_w, chans = field.shape
    patch_h, patch_w = blend_table.shape
    edge = 2 * MARGIN
    rows_n = lax.axis_size("row")
    cols_n = lax.axis_size("col")
    row_at = lax.axis_index("row")
    col_at = lax.axis_index("col")
    table_f = blend_table.astype(jnp.float32)
    grown = extended(field, (("row", 0), ("col", 1)), edge)
    own_shift = offsets[row_at, col_at]
    start_r = MARGIN + own_shift[0]
    start_c = MARGIN + own_shift[1]
    zero = jnp.int32(0)
    patch = lax.dynamic_slice(grown, (start_r, start_c, zero), (patch_h, patch_w, chans))
    out_patch, back = jax.vjp(patch_net, patch, w_first, w_down, w_up)
    empty = jnp.zeros((tile_h + 2 * edge, tile_w + 2 * edge, chans), jnp.float32)
    canvas = lax.dynamic_update_slice(
        empty, table_f[:, :, None] * out_patch, (start_r, start_c, zero)
    )
    numer = return_margins(canvas, tile_h, tile_w, edge)
    weight_sum = weight_total(
        offsets, table_f, row_at, col_at, rows_n, cols_n, tile_h, tile_w, 0, 1
    )
    ratio = cotangent.astype(jnp.float32) / weight_sum[:, :, None]
    ratio_grown = extended(ratio.astype(jnp.bfloat16), (("row", 0), ("col", 1)), edge).astype(
        ratio.dtype
    )
    blended = (numer / weight_sum[:, :, None]).astype(jnp.bfloat16)
    out_grad = table_f[:, :, None] * lax.dynamic_slice(
        ratio_grown, (start_r, start_c, zero), (patch_h, patch_w, chans)
    )
    d_patch, d_first, d_down, d_up = back(out_grad)
    d_canvas = lax.dynamic_update_slice(
        empty, d_patch.astype(jnp.float32), (start_r, start_c, zero)
    )
    field_grad = return_margins(d_canvas, tile_h, tile_w, edge)
    g_first, g_down, g_up = lax.psum(
        (d_first.astype(jnp.float32), d_down.astype(jnp.float32), d_up.astype(jnp.float32)),
        ("col", "row"),
    )
    scale = 1.0 / math.sqrt(tile_h * rows_n * tile_w * cols_n)
    return (blended, field_grad, g_first * scale, g_down * scale, g_up * scale)


def solution(mesh):
    return jax.shard_map(
        per_device,
        mesh=mesh,
        in_specs=(P("row", "col", None), P("row", "col", None), P(), P(), P(), P(), P()),
        out_specs=(P("row", "col", None), P("row", "col", None), P(), P(), P()),
        check_vma=False,
    )
```

profile of v0, /device:TPU:17, one launch (start us, length us, event | category | flops | bytes accessed | tf_op | source)
XLA Modules:
  0.0 498.5 jit_solution(4310469566527345241)
XLA Ops:
  7.2 10.6 %collective-permute-start = (bf16[16,16,128]{2,1,0:T(8,128)(2,1)}, bf16[16,16,128]{2,1,0:T(8,128)(2,1)S(1)}, u32[]{:S(2)}, u32[]{:S(2)}) collective-permute-start(bf16[16,16,128]{2,1,0:T(8,128)(2,1)} %param.23), channel_id=1, source_target_pairs={{0,1},{1,2},{2,3},{3,4},{4,5},{5,6},{6,7},{8,9},{9,10},{10,11},{11... | collective-permute-start | bytes 196616 | tf_op jit(solution)/shard_map/ppermute | solution.py:23
  17.9 1.3 collective-permute-start.1
  19.2 1.0 constant_dynamic-slice_fusion
  23.4 0.9 fusion.167
  24.3 0.9 fusion.168
  26.5 0.9 fusion.169
  29.4 0.9 fusion.170
  31.7 0.9 fusion.171
  34.5 0.9 fusion.172
  36.8 0.9 fusion.173
  39.6 0.9 fusion.174
  41.9 0.9 fusion.175
  45.4 3.9 collective-permute-start.2
  49.3 1.9 collective-permute-start.3
  51.4 8.1 %collective-permute-start.8 = (bf16[16,16,128]{2,1,0:T(8,128)(2,1)S(1)}, bf16[16,16,128]{2,1,0:T(8,128)(2,1)S(1)}, u32[]{:S(2)}, u32[]{:S(2)}) collective-permute-start(bf16[16,16,128]{2,1,0:T(8,128)(2,1)S(1)} %divide_convert_fusion), channel_id=1, source_target_pairs={{0,1},{1,2},{2,3},{3,4},{4,5},{5,6},{6,7},{8,9},{9,10},{10,11},{11... | collective-permute-start | bytes 196616 | tf_op jit(solution)/shard_map/ppermute | solution.py:23
  59.5 1.3 collective-permute-start.9
  63.4 5.0 %collective-permute-done.9 = bf16[16,16,128]{2,1,0:T(8,128)(2,1)S(1)} collective-permute-done((bf16[16,16,128]{2,1,0:T(8,128)(2,1)S(1)}, bf16[16,16,128]{2,1,0:T(8,128)(2,1)S(1)}, u32[]{:S(2)}, u32[]{:S(2)}) %collective-permute-start.9) | collective-permute-done | bytes 65568 | tf_op jit(solution)/shard_map/ppermute | solution.py:24
  69.2 5.7 %collective-permute-start.10 = (bf16[48,16,128]{2,1,0:T(8,128)(2,1)}, bf16[48,16,128]{2,1,0:T(8,128)(2,1)}, u32[]{:S(2)}, u32[]{:S(2)}) collective-permute-start(bf16[48,16,128]{2,1,0:T(8,128)(2,1)} %pad_maximum_fusion.1), channel_id=1, source_target_pairs={{0,8},{8,16},{16,24},{24,32},{32,40},{40,48},{48,56},{56,64},{64,7... | collective-permute-start | bytes 589832 | tf_op jit(solution)/shard_map/ppermute | solution.py:23
  74.9 2.8 collective-permute-start.11
  88.6 2.3 convert_multiply_fusion.2
  91.1 0.9 fusion.14
  92.2 0.9 fusion.13
  93.3 0.9 fusion.15
  94.1 0.8 fusion.16
  97.0 0.8 fusion.24
  97.8 0.8 fusion.23
  99.5 0.8 fusion.21
  100.3 0.8 fusion.20
  107.4 5.6 %pad.156 = bf16[34,34,128]{2,1,0:T(8,128)(2,1)S(1)} pad(bf16[16,16,128]{2,1,0:T(8,128)(2,1)} %bitcast.505, bf16[]{:T(256)} %constant.241.clone.1), padding=2_1_1x0_3_1x0_0_0 | pad | bytes 361474 | tf_op jit(solution)/shard_map/transpose(jvp())/pad | solution.py:52
  113.0 8.5 %pad.345 = bf16[33,33,128]{2,1,0:T(8,128)(2,1)} pad(bf16[16,16,128]{2,1,0:T(8,128)(2,1)} %bitcast.504, bf16[]{:T(256)} %constant.241.clone.1), padding=0_2_1x0_2_1x0_0_0 | pad | bytes 344322
  121.5 8.5 %pad.348 = bf16[32,33,128]{2,1,0:T(8,128)(2,1)} pad(bf16[16,16,128]{2,1,0:T(8,128)(2,1)} %bitcast.511, bf16[]{:T(256)} %constant.241.clone.1), padding=0_1_1x0_2_1x0_0_0 | pad | bytes 335874
  130.0 8.4 %pad.346 = bf16[33,32,128]{2,1,0:T(8,128)(2,1)} pad(bf16[16,16,128]{2,1,0:T(8,128)(2,1)} %bitcast.510, bf16[]{:T(256)} %constant.241.clone.1), padding=0_2_1x0_1_1x0_0_0 | pad | bytes 335874
  138.4 8.4 %pad.347 = bf16[33,32,128]{2,1,0:T(8,128)(2,1)} pad(bf16[16,16,128]{2,1,0:T(8,128)(2,1)} %bitcast.509, bf16[]{:T(256)} %constant.241.clone.1), padding=0_2_1x1_0_1x0_0_0 | pad | bytes 335874
  146.8 8.4 %pad.214 = bf16[32,32,128]{2,1,0:T(8,128)(2,1)} pad(bf16[16,16,128]{2,1,0:T(8,128)(2,1)} %bitcast.503, bf16[]{:T(256)} %constant.241.clone.1), padding=0_1_1x1_0_1x0_0_0 | pad | bytes 327682 | tf_op jit(solution)/shard_map/transpose(jvp(jit(_pad)))/pad | solution.py:46
  155.2 5.6 %pad.215 = bf16[32,32,128]{2,1,0:T(8,128)(2,1)} pad(bf16[16,16,128]{2,1,0:T(8,128)(2,1)S(1)} %bitcast.502, bf16[]{:T(256)} %constant.241.clone.1), padding=0_1_1x0_1_1x0_0_0 | pad | bytes 327682 | tf_op jit(solution)/shard_map/transpose(jvp(jit(_pad)))/pad | solution.py:46
  160.8 0.9 copy-done.2
  162.0 1.7 fusion.52
  164.5 0.9 fusion.38
  165.4 0.9 fusion.39
  166.3 0.9 fusion.40
  167.2 0.9 fusion.41
  168.1 0.9 fusion.42
  168.9 0.9 fusion.43
  172.8 1.3 dynamic_update_slice.7
  174.9 4.2 collective-permute-start.12
  179.1 1.3 collective-permute-start.13
  180.4 1.3 dynamic_update_slice.6
  182.7 8.6 %collective-permute-start.4 = (bf16[16,48,128]{2,1,0:T(8,128)(2,1)}, bf16[16,48,128]{2,1,0:T(8,128)(2,1)}, u32[]{:S(2)}, u32[]{:S(2)}) collective-permute-start(bf16[16,48,128]{2,1,0:T(8,128)(2,1)} %get-tuple-element.110), channel_id=1, source_target_pairs={{0,1},{1,2},{2,3},{3,4},{4,5},{5,6},{6,7},{8,9},{9,10},{10,11},{11... | collective-permute-start | bytes 589832 | tf_op jit(solution)/shard_map/ppermute | solution.py:13
  191.2 1.3 collective-permute-start.5
  192.5 0.8 add_convert_fusion.2
  193.4 0.9 add_convert_fusion.1
  194.6 1.2 add_convert_fusion
  195.8 11.9 %collective-permute-done.5 = bf16[16,48,128]{2,1,0:T(8,128)(2,1)} collective-permute-done((bf16[16,48,128]{2,1,0:T(8,128)(2,1)S(1)}, bf16[16,48,128]{2,1,0:T(8,128)(2,1)}, u32[]{:S(2)}, u32[]{:S(2)}) %collective-permute-start.5) | collective-permute-done | bytes 196640 | tf_op jit(solution)/shard_map/ppermute | solution.py:13
  207.6 1.1 fusion.205
  208.7 12.5 %collective-permute-start.6 = (bf16[16,16,128]{2,1,0:T(8,128)(2,1)S(1)}, bf16[16,16,128]{2,1,0:T(8,128)(2,1)S(1)}, u32[]{:S(2)}, u32[]{:S(2)}) collective-permute-start(bf16[16,16,128]{2,1,0:T(8,128)(2,1)S(1)} %get-tuple-element.128), channel_id=1, source_target_pairs={{0,8},{8,16},{16,24},{24,32},{32,40},{40,48},{48,56},{56,64},{64,7... | collective-permute-start | bytes 196616 | tf_op jit(solution)/shard_map/ppermute | solution.py:13
  221.3 1.9 collective-permute-start.7
  223.2 1.1 fusion.203
  224.3 3.6 collective-permute-start.14
  228.0 1.9 collective-permute-start.15
  230.7 3.3 collective-permute-done.15
  234.7 252.5 %all-reduce.45.cloned.1.call-done = (f32[3,3,128,128]{3,2,1,0:T(8,128)}, f32[3,3,128,256]{3,2,1,0:T(8,128)}, f32[2,2,256,128]{3,2,1,0:T(8,128)}) async-done(((f32[3,3,128,128]{3,2,1,0:T(8,128)}, f32[3,3,128,256]{3,2,1,0:T(8,128)}, f32[2,2,256,128]{3,2,1,0:T(8,128)}), (f32[3,3,128,128]{3,2,1,0:T(8,128)}, f32[3,3,128,256]{3,2,1,0:T(8,128)}, f32[2,2,256,128]{3,2,1,0:T(8,128)})) %all-reduce.45.cloned.1.call-update) | async-done | bytes 2293776 | tf_op jit(solution)/shard_map/psum | solution.py:171
  487.1 2.4 broadcast_multiply_fusion
  489.6 0.9 broadcast_multiply_fusion.1
  490.8 0.8 broadcast_multiply_fusion.2
  (228 shorter events, 33.6 us)
Async XLA Ops:
  7.2 38.1 %copy-start.35 = (bf16[16,16,128]{2,1,0:T(8,128)(2,1)S(1)}, bf16[16,16,128]{2,1,0:T(8,128)(2,1)}, u32[]{:S(2)}) copy-start(bf16[16,16,128]{2,1,0:T(8,128)(2,1)} %param.23) | copy-start | bytes 196612
  7.2 56.2 %copy-start.43 = (s32[32,32]{1,0:T(8,128)S(1)}, s32[32,32]{1,0:T(8,128)}, u32[]{:S(2)}) copy-start(s32[32,32]{1,0:T(8,128)} %param.29) | copy-start | bytes 12292
  7.2 44.1 %copy-start.36 = (bf16[16,16,128]{2,1,0:T(8,128)(2,1)S(1)}, bf16[16,16,128]{2,1,0:T(8,128)(2,1)}, u32[]{:S(2)}) copy-start(bf16[16,16,128]{2,1,0:T(8,128)(2,1)} %param.24) | copy-start | bytes 196612
  7.2 479.9 %all-reduce.45.cloned.1.call-start = ((), (), s32[]{:S(2)}) async-start(), calls=%async_computation | async-start | bytes 4587520 | tf_op jit(solution)/shard_map/psum | solution.py:171
  7.2 38.0 %collective-permute-start = (bf16[16,16,128]{2,1,0:T(8,128)(2,1)}, bf16[16,16,128]{2,1,0:T(8,128)(2,1)S(1)}, u32[]{:S(2)}, u32[]{:S(2)}) collective-permute-start(bf16[16,16,128]{2,1,0:T(8,128)(2,1)} %param.23), channel_id=1, source_target_pairs={{0,1},{1,2},{2,3},{3,4},{4,5},{5,6},{6,7},{8,9},{9,10},{10,11},{11... | collective-permute-start | bytes 196616 | tf_op jit(solution)/shard_map/ppermute | solution.py:23
  17.9 27.5 %collective-permute-start.1 = (bf16[16,16,128]{2,1,0:T(8,128)(2,1)}, bf16[16,16,128]{2,1,0:T(8,128)(2,1)S(1)}, u32[]{:S(2)}, u32[]{:S(2)}) collective-permute-start(bf16[16,16,128]{2,1,0:T(8,128)(2,1)} %param.23), channel_id=1, source_target_pairs={{1,0},{2,1},{3,2},{4,3},{5,4},{6,5},{7,6},{9,8},{10,9},{11,10},{12... | collective-permute-start | bytes 196616 | tf_op jit(solution)/shard_map/ppermute | solution.py:24
  45.4 32.4 %collective-permute-start.2 = (bf16[48,16,128]{2,1,0:T(8,128)(2,1)S(1)}, bf16[48,16,128]{2,1,0:T(8,128)(2,1)S(1)}, u32[]{:S(2)}, u32[]{:S(2)}) collective-permute-start(bf16[48,16,128]{2,1,0:T(8,128)(2,1)S(1)} %constant_dynamic-update-slice_fusion), channel_id=1, source_target_pairs={{0,8},{8,16},{16,24},{24,32},{32,40},{40,48},{48,56},{56,64},{64,7... | collective-permute-start | bytes 589832 | tf_op jit(solution)/shard_map/ppermute | solution.py:23
  49.3 28.4 %collective-permute-start.3 = (bf16[48,16,128]{2,1,0:T(8,128)(2,1)S(1)}, bf16[48,16,128]{2,1,0:T(8,128)(2,1)S(1)}, u32[]{:S(2)}, u32[]{:S(2)}) collective-permute-start(bf16[48,16,128]{2,1,0:T(8,128)(2,1)S(1)} %constant_dynamic-update-slice_fusion), channel_id=1, source_target_pairs={{8,0},{16,8},{24,16},{32,24},{40,32},{48,40},{56,48},{64,56},{72,6... | collective-permute-start | bytes 589832 | tf_op jit(solution)/shard_map/ppermute | solution.py:24
  51.4 12.0 %collective-permute-start.8 = (bf16[16,16,128]{2,1,0:T(8,128)(2,1)S(1)}, bf16[16,16,128]{2,1,0:T(8,128)(2,1)S(1)}, u32[]{:S(2)}, u32[]{:S(2)}) collective-permute-start(bf16[16,16,128]{2,1,0:T(8,128)(2,1)S(1)} %divide_convert_fusion), channel_id=1, source_target_pairs={{0,1},{1,2},{2,3},{3,4},{4,5},{5,6},{6,7},{8,9},{9,10},{10,11},{11... | collective-permute-start | bytes 196616 | tf_op jit(solution)/shard_map/ppermute | solution.py:23
  59.5 9.0 %collective-permute-start.9 = (bf16[16,16,128]{2,1,0:T(8,128)(2,1)S(1)}, bf16[16,16,128]{2,1,0:T(8,128)(2,1)S(1)}, u32[]{:S(2)}, u32[]{:S(2)}) collective-permute-start(bf16[16,16,128]{2,1,0:T(8,128)(2,1)S(1)} %divide_convert_fusion), channel_id=1, source_target_pairs={{1,0},{2,1},{3,2},{4,3},{5,4},{6,5},{7,6},{9,8},{10,9},{11,10},{12... | collective-permute-start | bytes 196616 | tf_op jit(solution)/shard_map/ppermute | solution.py:24
  63.4 14.9 %copy-start.29 = (bf16[16,16,128]{2,1,0:T(8,128)(2,1)}, bf16[16,16,128]{2,1,0:T(8,128)(2,1)S(1)}, u32[]{:S(2)}) copy-start(bf16[16,16,128]{2,1,0:T(8,128)(2,1)S(1)} %collective-permute-done.8) | copy-start | bytes 196612
  68.5 9.9 %copy-start.31 = (bf16[16,16,128]{2,1,0:T(8,128)(2,1)}, bf16[16,16,128]{2,1,0:T(8,128)(2,1)S(1)}, u32[]{:S(2)}) copy-start(bf16[16,16,128]{2,1,0:T(8,128)(2,1)S(1)} %collective-permute-done.9) | copy-start | bytes 196612
  69.2 19.0 %collective-permute-start.10 = (bf16[48,16,128]{2,1,0:T(8,128)(2,1)}, bf16[48,16,128]{2,1,0:T(8,128)(2,1)}, u32[]{:S(2)}, u32[]{:S(2)}) collective-permute-start(bf16[48,16,128]{2,1,0:T(8,128)(2,1)} %pad_maximum_fusion.1), channel_id=1, source_target_pairs={{0,8},{8,16},{16,24},{24,32},{32,40},{40,48},{48,56},{56,64},{64,7... | collective-permute-start | bytes 589832 | tf_op jit(solution)/shard_map/ppermute | solution.py:23
  74.9 13.3 %collective-permute-start.11 = (bf16[48,16,128]{2,1,0:T(8,128)(2,1)}, bf16[48,16,128]{2,1,0:T(8,128)(2,1)}, u32[]{:S(2)}, u32[]{:S(2)}) collective-permute-start(bf16[48,16,128]{2,1,0:T(8,128)(2,1)} %pad_maximum_fusion.1), channel_id=1, source_target_pairs={{8,0},{16,8},{24,16},{32,24},{40,32},{48,40},{56,48},{64,56},{72,6... | collective-permute-start | bytes 589832 | tf_op jit(solution)/shard_map/ppermute | solution.py:24
  78.0 1.0 copy-start.1
  80.9 4.0 copy-start
  81.7 3.7 copy-start.16
  83.3 2.3 copy-start.8
  83.7 2.1 copy-start.10
  84.1 1.9 copy-start.12
  84.5 1.7 copy-start.14
  84.9 1.5 copy-start.33
  86.0 1.0 copy-start.6
  87.7 0.8 copy-start.30
  87.7 0.9 copy-start.32
  95.3 0.8 copy-start.34
  95.4 1.7 copy-start.15
  95.4 2.5 copy-start.13
  95.4 3.3 copy-start.11
  95.6 3.9 copy-start.9
  160.8 1.0 copy-start.2
  160.8 1.1 copy-start.3
  160.8 1.1 copy-start.4
  160.8 1.2 copy-start.5
  174.9 48.3 %collective-permute-start.12 = (bf16[16,48,128]{2,1,0:T(8,128)(2,1)}, bf16[16,48,128]{2,1,0:T(8,128)(2,1)}, u32[]{:S(2)}, u32[]{:S(2)}) collective-permute-start(bf16[16,48,128]{2,1,0:T(8,128)(2,1)} %get-tuple-element.108), channel_id=1, source_target_pairs={{0,1},{1,2},{2,3},{3,4},{4,5},{5,6},{6,7},{8,9},{9,10},{10,11},{11... | collective-permute-start | bytes 589832 | tf_op jit(solution)/shard_map/ppermute | solution.py:13
  179.1 44.1 %collective-permute-start.13 = (bf16[16,48,128]{2,1,0:T(8,128)(2,1)S(1)}, bf16[16,48,128]{2,1,0:T(8,128)(2,1)}, u32[]{:S(2)}, u32[]{:S(2)}) collective-permute-start(bf16[16,48,128]{2,1,0:T(8,128)(2,1)S(1)} %get-tuple-element.109), channel_id=1, source_target_pairs={{1,0},{2,1},{3,2},{4,3},{5,4},{6,5},{7,6},{9,8},{10,9},{11,10},{12... | collective-permute-start | bytes 589832 | tf_op jit(solution)/shard_map/ppermute | solution.py:13
  181.7 10.8 %copy-start.25 = (bf16[1,1,256,128]{3,2,1,0:T(8,128)(2,1)S(1)}, bf16[1,1,256,128]{3,2,1,0:T(8,128)(2,1)}, u32[]{:S(2)}) copy-start(bf16[1,1,256,128]{3,2,1,0:T(8,128)(2,1)} %fusion.14) | copy-start | bytes 196612
  181.7 10.8 %copy-start.26 = (bf16[1,1,256,128]{3,2,1,0:T(8,128)(2,1)S(1)}, bf16[1,1,256,128]{3,2,1,0:T(8,128)(2,1)}, u32[]{:S(2)}) copy-start(bf16[1,1,256,128]{3,2,1,0:T(8,128)(2,1)} %fusion.13) | copy-start | bytes 196612
  181.7 10.8 %copy-start.27 = (bf16[1,1,256,128]{3,2,1,0:T(8,128)(2,1)S(1)}, bf16[1,1,256,128]{3,2,1,0:T(8,128)(2,1)}, u32[]{:S(2)}) copy-start(bf16[1,1,256,128]{3,2,1,0:T(8,128)(2,1)} %fusion.15) | copy-start | bytes 196612
  181.7 10.8 %copy-start.28 = (bf16[1,1,256,128]{3,2,1,0:T(8,128)(2,1)S(1)}, bf16[1,1,256,128]{3,2,1,0:T(8,128)(2,1)}, u32[]{:S(2)}) copy-start(bf16[1,1,256,128]{3,2,1,0:T(8,128)(2,1)} %fusion.16) | copy-start | bytes 196612
  181.8 11.5 %copy-start.37 = (bf16[1,1,128,128]{3,2,1,0:T(8,128)(2,1)S(1)}, bf16[1,1,128,128]{3,2,1,0:T(8,128)(2,1)}, u32[]{:S(2)}) copy-start(bf16[1,1,128,128]{3,2,1,0:T(8,128)(2,1)} %fusion.38) | copy-start | bytes 98308
  181.9 11.5 %copy-start.38 = (bf16[1,1,128,128]{3,2,1,0:T(8,128)(2,1)S(1)}, bf16[1,1,128,128]{3,2,1,0:T(8,128)(2,1)}, u32[]{:S(2)}) copy-start(bf16[1,1,128,128]{3,2,1,0:T(8,128)(2,1)} %fusion.39) | copy-start | bytes 98308
  181.9 11.5 %copy-start.39 = (bf16[1,1,128,128]{3,2,1,0:T(8,128)(2,1)S(1)}, bf16[1,1,128,128]{3,2,1,0:T(8,128)(2,1)}, u32[]{:S(2)}) copy-start(bf16[1,1,128,128]{3,2,1,0:T(8,128)(2,1)} %fusion.40) | copy-start | bytes 98308
  181.9 11.5 %copy-start.40 = (bf16[1,1,128,128]{3,2,1,0:T(8,128)(2,1)S(1)}, bf16[1,1,128,128]{3,2,1,0:T(8,128)(2,1)}, u32[]{:S(2)}) copy-start(bf16[1,1,128,128]{3,2,1,0:T(8,128)(2,1)} %fusion.41) | copy-start | bytes 98308
  181.9 11.5 %copy-start.41 = (bf16[1,1,128,128]{3,2,1,0:T(8,128)(2,1)S(1)}, bf16[1,1,128,128]{3,2,1,0:T(8,128)(2,1)}, u32[]{:S(2)}) copy-start(bf16[1,1,128,128]{3,2,1,0:T(8,128)(2,1)} %fusion.42) | copy-start | bytes 98308
  181.9 11.5 %copy-start.42 = (bf16[1,1,128,128]{3,2,1,0:T(8,128)(2,1)S(1)}, bf16[1,1,128,128]{3,2,1,0:T(8,128)(2,1)}, u32[]{:S(2)}) copy-start(bf16[1,1,128,128]{3,2,1,0:T(8,128)(2,1)} %fusion.43) | copy-start | bytes 98308
  181.9 12.4 %copy-start.17 = (bf16[16,16,128]{2,1,0:T(8,128)(2,1)S(1)}, bf16[16,16,128]{2,1,0:T(8,128)(2,1)}, u32[]{:S(2)}) copy-start(bf16[16,16,128]{2,1,0:T(8,128)(2,1)} %copy-done.16) | copy-start | bytes 196612
  181.9 12.6 %copy-start.19 = (bf16[1,1,128,256]{3,2,1,0:T(8,128)(2,1)S(1)}, bf16[1,1,128,256]{3,2,1,0:T(8,128)(2,1)}, u32[]{:S(2)}) copy-start(bf16[1,1,128,256]{3,2,1,0:T(8,128)(2,1)} %fusion.25) | copy-start | bytes 196612
  181.9 12.6 %copy-start.20 = (bf16[1,1,128,256]{3,2,1,0:T(8,128)(2,1)S(1)}, bf16[1,1,128,256]{3,2,1,0:T(8,128)(2,1)}, u32[]{:S(2)}) copy-start(bf16[1,1,128,256]{3,2,1,0:T(8,128)(2,1)} %fusion.24) | copy-start | bytes 196612
  181.9 12.6 %copy-start.21 = (bf16[1,1,128,256]{3,2,1,0:T(8,128)(2,1)S(1)}, bf16[1,1,128,256]{3,2,1,0:T(8,128)(2,1)}, u32[]{:S(2)}) copy-start(bf16[1,1,128,256]{3,2,1,0:T(8,128)(2,1)} %fusion.23) | copy-start | bytes 196612
  182.0 12.6 %copy-start.22 = (bf16[1,1,128,256]{3,2,1,0:T(8,128)(2,1)S(1)}, bf16[1,1,128,256]{3,2,1,0:T(8,128)(2,1)}, u32[]{:S(2)}) copy-start(bf16[1,1,128,256]{3,2,1,0:T(8,128)(2,1)} %fusion.22) | copy-start | bytes 196612
  182.0 12.6 %copy-start.23 = (bf16[1,1,128,256]{3,2,1,0:T(8,128)(2,1)S(1)}, bf16[1,1,128,256]{3,2,1,0:T(8,128)(2,1)}, u32[]{:S(2)}) copy-start(bf16[1,1,128,256]{3,2,1,0:T(8,128)(2,1)} %fusion.21) | copy-start | bytes 196612
  182.0 12.6 %copy-start.24 = (bf16[1,1,128,256]{3,2,1,0:T(8,128)(2,1)S(1)}, bf16[1,1,128,256]{3,2,1,0:T(8,128)(2,1)}, u32[]{:S(2)}) copy-start(bf16[1,1,128,256]{3,2,1,0:T(8,128)(2,1)} %fusion.20) | copy-start | bytes 196612
  182.7 13.1 %collective-permute-start.4 = (bf16[16,48,128]{2,1,0:T(8,128)(2,1)}, bf16[16,48,128]{2,1,0:T(8,128)(2,1)}, u32[]{:S(2)}, u32[]{:S(2)}) collective-permute-start(bf16[16,48,128]{2,1,0:T(8,128)(2,1)} %get-tuple-element.110), channel_id=1, source_target_pairs={{0,1},{1,2},{2,3},{3,4},{4,5},{5,6},{6,7},{8,9},{9,10},{10,11},{11... | collective-permute-start | bytes 589832 | tf_op jit(solution)/shard_map/ppermute | solution.py:13
  191.2 16.4 %collective-permute-start.5 = (bf16[16,48,128]{2,1,0:T(8,128)(2,1)S(1)}, bf16[16,48,128]{2,1,0:T(8,128)(2,1)}, u32[]{:S(2)}, u32[]{:S(2)}) collective-permute-start(bf16[16,48,128]{2,1,0:T(8,128)(2,1)S(1)} %get-tuple-element.111), channel_id=1, source_target_pairs={{1,0},{2,1},{3,2},{4,3},{5,4},{6,5},{7,6},{9,8},{10,9},{11,10},{12... | collective-permute-start | bytes 589832 | tf_op jit(solution)/shard_map/ppermute | solution.py:13
  208.7 21.2 %collective-permute-start.6 = (bf16[16,16,128]{2,1,0:T(8,128)(2,1)S(1)}, bf16[16,16,128]{2,1,0:T(8,128)(2,1)S(1)}, u32[]{:S(2)}, u32[]{:S(2)}) collective-permute-start(bf16[16,16,128]{2,1,0:T(8,128)(2,1)S(1)} %get-tuple-element.128), channel_id=1, source_target_pairs={{0,8},{8,16},{16,24},{24,32},{32,40},{40,48},{48,56},{56,64},{64,7... | collective-permute-start | bytes 196616 | tf_op jit(solution)/shard_map/ppermute | solution.py:13
  221.3 8.7 %collective-permute-start.7 = (bf16[16,16,128]{2,1,0:T(8,128)(2,1)S(1)}, bf16[16,16,128]{2,1,0:T(8,128)(2,1)S(1)}, u32[]{:S(2)}, u32[]{:S(2)}) collective-permute-start(bf16[16,16,128]{2,1,0:T(8,128)(2,1)S(1)} %get-tuple-element.129), channel_id=1, source_target_pairs={{8,0},{16,8},{24,16},{32,24},{40,32},{48,40},{56,48},{64,56},{72,6... | collective-permute-start | bytes 196616 | tf_op jit(solution)/shard_map/ppermute | solution.py:13
  224.3 6.3 %collective-permute-start.14 = (bf16[16,16,128]{2,1,0:T(8,128)(2,1)S(1)}, bf16[16,16,128]{2,1,0:T(8,128)(2,1)S(1)}, u32[]{:S(2)}, u32[]{:S(2)}) collective-permute-start(bf16[16,16,128]{2,1,0:T(8,128)(2,1)S(1)} %get-tuple-element.126), channel_id=1, source_target_pairs={{0,8},{8,16},{16,24},{24,32},{32,40},{40,48},{48,56},{56,64},{64,7... | collective-permute-start | bytes 196616 | tf_op jit(solution)/shard_map/ppermute | solution.py:13
  228.0 6.0 %collective-permute-start.15 = (bf16[16,16,128]{2,1,0:T(8,128)(2,1)S(1)}, bf16[16,16,128]{2,1,0:T(8,128)(2,1)S(1)}, u32[]{:S(2)}, u32[]{:S(2)}) collective-permute-start(bf16[16,16,128]{2,1,0:T(8,128)(2,1)S(1)} %get-tuple-element.127), channel_id=1, source_target_pairs={{8,0},{16,8},{24,16},{32,24},{40,32},{48,40},{56,48},{64,56},{72,6... | collective-permute-start | bytes 196616 | tf_op jit(solution)/shard_map/ppermute | solution.py:13
  487.1 2.5 copy-start.7
  489.6 1.3 copy-start.18
Sparse Core Ops, SparseCore 0:
  195.9 291.1 all-reduce.44
where the time goes:
time: 502 us; the launch traced here: 499 us
  waiting for transfers between devices  273 us (54%)
  starting transfers between devices  71.1 us (14%)
  local copies, waits for them, and re-layouts  70.1 us (14%)
  matrix products  37.5 us (7%)
  between operations  30.1 us (6%)
  other arithmetic  17.1 us (3%)
    psum x1, waiting for transfers between devices, per_device(): lax.psum((d_first.astype(jnp.float32), d_down.astype(jnp.float32), d_up.a...  252 us
    unnamed x94, local copies, waits for them, and re-layouts  37.2 us
    ppermute x8, starting transfers between devices, passed_along(): return lax.ppermute(block, axis, route)  35.3 us
    ppermute x4, starting transfers between devices, extended(): before = lax.ppermute(last, axis, up)  28.4 us
    ppermute x8, waiting for transfers between devices, passed_along(): return lax.ppermute(block, axis, route)  15.2 us
    pad x3, local copies, waits for them, and re-layouts, conv_down(): padded = jnp.pad(inputs, ((1, 1), (1, 1), (0, 0)))  14.1 us
    dot_general x27, matrix products, conv_down(): jnp.dot(window, kernel[row_tap, col_tap], preferred_element_type=jnp.floa...  12.5 us
    dot_general x27, matrix products, conv_same(): jnp.dot(window, kernel[row_tap, col_tap], preferred_element_type=jnp.floa...  10.1 us
  transfers between devices with their start and end apart: 17, of which 4 were waited for; matrix products, arithmetic and copies ran while one was open for 7% of the time, Pallas kernels for 0%

commit v1 on v0

--- a/solution.py
+++ b/solution.py
@@ -169,8 +169,11 @@
     )
     field_grad = return_margins(d_canvas, tile_h, tile_w, edge)
     g_first, g_down, g_up = lax.psum(
-        (d_first.astype(jnp.float32), d_down.astype(jnp.float32), d_up.astype(jnp.float32)),
-        ("col", "row"),
+        lax.psum(
+            (d_first.astype(jnp.float32), d_down.astype(jnp.float32), d_up.astype(jnp.float32)),
+            "row",
+        ),
+        "col",
     )
     scale = 1.0 / math.sqrt(tile_h * rows_n * tile_w * cols_n)
     return (blended, field_grad, g_first * scale, g_down * scale, g_up * scale)

time: 502 us -> 936 us (1.86)
  the two profiles are of different devices: /device:TPU:17 before, /device:TPU:2 now
where the time goes in v1:
time: 936 us; the launch traced here: 934 us
  waiting for transfers between devices  743 us (79%)
  starting transfers between devices  56.9 us (6%)
  local copies, waits for them, and re-layouts  54.4 us (6%)
  matrix products  33.8 us (4%)
  between operations  29.6 us (3%)
  other arithmetic  16.2 us (2%)
    psum x1, waiting for transfers between devices, per_device(): lax.psum(lax.psum((d_first.astype(jnp.float32), d_down.astype(jnp.float32...  497 us
    psum x1, waiting for transfers between devices, per_device(): lax.psum((d_first.astype(jnp.float32), d_down.astype(jnp.float32), d_up.a...  220 us
    unnamed x82, local copies, waits for them, and re-layouts  31.7 us
    ppermute x8, starting transfers between devices, passed_along(): return lax.ppermute(block, axis, route)  26.5 us
    ppermute x4, starting transfers between devices, extended(): before = lax.ppermute(last, axis, up)  22.7 us
    ppermute x8, waiting for transfers between devices, passed_along(): return lax.ppermute(block, axis, route)  19.4 us
  transfers between devices with their start and end apart: 18, of which 7 were waited for; matrix products, arithmetic and copies ran while one was open for 3% of the time, Pallas kernels for 0%

profile of v1, /device:TPU:2, one launch (start us, length us, event | category | flops | bytes accessed | tf_op | source)
XLA Modules:
  0.0 933.9 jit_solution(15904743447958515720)
XLA Ops:
  7.2 10.9 %collective-permute-start = (bf16[16,16,128]{2,1,0:T(8,128)(2,1)}, bf16[16,16,128]{2,1,0:T(8,128)(2,1)S(1)}, u32[]{:S(2)}, u32[]{:S(2)}) collective-permute-start(bf16[16,16,128]{2,1,0:T(8,128)(2,1)} %param.23), channel_id=1, source_target_pairs={{0,1},{1,2},{2,3},{3,4},{4,5},{5,6},{6,7},{8,9},{9,10},{10,11},{11... | collective-permute-start | bytes 196616 | tf_op jit(solution)/shard_map/ppermute | solution.py:23
  18.2 1.9 collective-permute-start.1
  20.1 1.0 constant_dynamic-slice_fusion
  24.1 0.9 fusion.167
  25.0 0.9 fusion.168
  27.2 0.9 fusion.169
  30.0 0.9 fusion.170
  32.1 0.9 fusion.171
  34.9 0.9 fusion.172
  37.1 0.9 fusion.173
  39.8 0.9 fusion.174
  42.0 0.9 fusion.175
  45.5 1.5 collective-permute-start.2
  47.0 1.3 collective-permute-start.3
  48.4 7.7 collective-permute-start.8
  56.1 3.0 collective-permute-start.9
  61.7 6.3 collective-permute-done.9
  68.8 2.6 collective-permute-start.10
  71.4 1.3 collective-permute-start.11
  83.3 2.3 convert_multiply_fusion.2
  85.9 0.9 fusion.14
  86.9 0.9 fusion.13
  88.0 0.9 fusion.15
  88.9 0.9 fusion.16
  91.0 0.8 fusion.25
  91.8 0.8 fusion.24
  92.8 0.8 fusion.22
  93.7 0.8 fusion.21
  94.5 0.8 fusion.20
  96.1 0.8 fusion.18
  97.0 0.8 fusion.17
  98.5 0.8 convolution_convert_fusion.20
  102.0 5.6 pad.345
  107.6 8.5 pad.348
  116.1 8.4 pad.346
  124.5 5.6 pad.347
  130.1 5.6 pad.214
  135.7 5.6 pad.215
  141.3 0.9 copy-done.2
  142.3 1.8 fusion.52
  147.0 0.8 add_convert_fusion.2
  147.9 1.2 add_convert_fusion
  149.0 0.9 add_convert_fusion.1
  150.6 0.9 convolution_convert_fusion.6
  152.7 220.4 %all-reduce.49.cloned.1.call-done = (f32[3,3,128,128]{3,2,1,0:T(8,128)}, f32[3,3,128,256]{3,2,1,0:T(8,128)}, f32[2,2,256,128]{3,2,1,0:T(8,128)}) async-done(((f32[3,3,128,128]{3,2,1,0:T(8,128)}, f32[3,3,128,256]{3,2,1,0:T(8,128)}, f32[2,2,256,128]{3,2,1,0:T(8,128)}), (f32[3,3,128,128]{3,2,1,0:T(8,128)}, f32[3,3,128,256]{3,2,1,0:T(8,128)}, f32[2,2,256,128]{3,2,1,0:T(8,128)})) %all-reduce.49.cloned.1.call-update) | async-done | bytes 2293776 | tf_op jit(solution)/shard_map/psum | solution.py:172
  373.4 1.2 pad_add_fusion
  375.2 1.3 dynamic_update_slice.7
  376.7 1.3 dynamic_update_slice.6
  378.1 4.6 collective-permute-start.4
  382.7 6.0 collective-permute-start.5
  388.8 3.7 collective-permute-start.12
  392.5 6.9 collective-permute-start.13
  399.4 1.2 collective-permute-done.5
  400.7 1.3 collective-permute-start.6
  402.0 1.3 collective-permute-start.7
  403.3 8.6 collective-permute-done.12
  411.9 2.1 collective-permute-done.13
  414.1 1.3 collective-permute-start.14
  415.5 1.3 collective-permute-start.15
  417.5 7.5 collective-permute-done.15
  425.7 496.9 %all-reduce.47.cloned.1.call-done = (f32[3,3,128,128]{3,2,1,0:T(8,128)}, f32[3,3,128,256]{3,2,1,0:T(8,128)}, f32[2,2,256,128]{3,2,1,0:T(8,128)}) async-done(((f32[3,3,128,128]{3,2,1,0:T(8,128)}, f32[3,3,128,256]{3,2,1,0:T(8,128)}, f32[2,2,256,128]{3,2,1,0:T(8,128)}), (f32[3,3,128,128]{3,2,1,0:T(8,128)}, f32[3,3,128,256]{3,2,1,0:T(8,128)}, f32[2,2,256,128]{3,2,1,0:T(8,128)})) %all-reduce.47.cloned.1.call-update) | async-done | bytes 2293776 | tf_op jit(solution)/shard_map/psum | solution.py:171
  922.5 2.4 broadcast_multiply_fusion
  925.0 0.9 broadcast_multiply_fusion.1
  926.2 0.8 broadcast_multiply_fusion.2
  (219 shorter events, 29.7 us)
Async XLA Ops:
  7.2 38.3 %copy-start.35 = (bf16[16,16,128]{2,1,0:T(8,128)(2,1)S(1)}, bf16[16,16,128]{2,1,0:T(8,128)(2,1)}, u32[]{:S(2)}) copy-start(bf16[16,16,128]{2,1,0:T(8,128)(2,1)} %param.23) | copy-start | bytes 196612
  7.2 54.5 %copy-start.37 = (s32[32,32]{1,0:T(8,128)S(1)}, s32[32,32]{1,0:T(8,128)}, u32[]{:S(2)}) copy-start(s32[32,32]{1,0:T(8,128)} %param.29) | copy-start | bytes 12292
  7.2 41.1 %copy-start.36 = (bf16[16,16,128]{2,1,0:T(8,128)(2,1)S(1)}, bf16[16,16,128]{2,1,0:T(8,128)(2,1)}, u32[]{:S(2)}) copy-start(bf16[16,16,128]{2,1,0:T(8,128)(2,1)} %param.24) | copy-start | bytes 196612
  7.2 365.9 %all-reduce.49.cloned.1.call-start = ((), (), s32[]{:S(2)}) async-start(), calls=%async_computation.1 | async-start | bytes 4587520 | tf_op jit(solution)/shard_map/psum | solution.py:172
  7.2 38.2 %collective-permute-start = (bf16[16,16,128]{2,1,0:T(8,128)(2,1)}, bf16[16,16,128]{2,1,0:T(8,128)(2,1)S(1)}, u32[]{:S(2)}, u32[]{:S(2)}) collective-permute-start(bf16[16,16,128]{2,1,0:T(8,128)(2,1)} %param.23), channel_id=1, source_target_pairs={{0,1},{1,2},{2,3},{3,4},{4,5},{5,6},{6,7},{8,9},{9,10},{10,11},{11... | collective-permute-start | bytes 196616 | tf_op jit(solution)/shard_map/ppermute | solution.py:23
  18.2 27.3 %collective-permute-start.1 = (bf16[16,16,128]{2,1,0:T(8,128)(2,1)}, bf16[16,16,128]{2,1,0:T(8,128)(2,1)S(1)}, u32[]{:S(2)}, u32[]{:S(2)}) collective-permute-start(bf16[16,16,128]{2,1,0:T(8,128)(2,1)} %param.23), channel_id=1, source_target_pairs={{1,0},{2,1},{3,2},{4,3},{5,4},{6,5},{7,6},{9,8},{10,9},{11,10},{12... | collective-permute-start | bytes 196616 | tf_op jit(solution)/shard_map/ppermute | solution.py:24
  45.5 27.2 %collective-permute-start.2 = (bf16[48,16,128]{2,1,0:T(8,128)(2,1)S(1)}, bf16[48,16,128]{2,1,0:T(8,128)(2,1)S(1)}, u32[]{:S(2)}, u32[]{:S(2)}) collective-permute-start(bf16[48,16,128]{2,1,0:T(8,128)(2,1)S(1)} %constant_dynamic-update-slice_fusion), channel_id=1, source_target_pairs={{0,8},{8,16},{16,24},{24,32},{32,40},{40,48},{48,56},{56,64},{64,7... | collective-permute-start | bytes 589832 | tf_op jit(solution)/shard_map/ppermute | solution.py:23
  47.0 25.7 %collective-permute-start.3 = (bf16[48,16,128]{2,1,0:T(8,128)(2,1)S(1)}, bf16[48,16,128]{2,1,0:T(8,128)(2,1)S(1)}, u32[]{:S(2)}, u32[]{:S(2)}) collective-permute-start(bf16[48,16,128]{2,1,0:T(8,128)(2,1)S(1)} %constant_dynamic-update-slice_fusion), channel_id=1, source_target_pairs={{8,0},{16,8},{24,16},{32,24},{40,32},{48,40},{56,48},{64,56},{72,6... | collective-permute-start | bytes 589832 | tf_op jit(solution)/shard_map/ppermute | solution.py:24
  48.4 13.3 %collective-permute-start.8 = (bf16[16,16,128]{2,1,0:T(8,128)(2,1)S(1)}, bf16[16,16,128]{2,1,0:T(8,128)(2,1)S(1)}, u32[]{:S(2)}, u32[]{:S(2)}) collective-permute-start(bf16[16,16,128]{2,1,0:T(8,128)(2,1)S(1)} %divide_convert_fusion), channel_id=1, source_target_pairs={{0,1},{1,2},{2,3},{3,4},{4,5},{5,6},{6,7},{8,9},{9,10},{10,11},{11... | collective-permute-start | bytes 196616 | tf_op jit(solution)/shard_map/ppermute | solution.py:23
  56.1 12.0 %collective-permute-start.9 = (bf16[16,16,128]{2,1,0:T(8,128)(2,1)S(1)}, bf16[16,16,128]{2,1,0:T(8,128)(2,1)S(1)}, u32[]{:S(2)}, u32[]{:S(2)}) collective-permute-start(bf16[16,16,128]{2,1,0:T(8,128)(2,1)S(1)} %divide_convert_fusion), channel_id=1, source_target_pairs={{1,0},{2,1},{3,2},{4,3},{5,4},{6,5},{7,6},{9,8},{10,9},{11,10},{12... | collective-permute-start | bytes 196616 | tf_op jit(solution)/shard_map/ppermute | solution.py:24
  61.7 11.6 %copy-start.28 = (bf16[16,16,128]{2,1,0:T(8,128)(2,1)}, bf16[16,16,128]{2,1,0:T(8,128)(2,1)S(1)}, u32[]{:S(2)}) copy-start(bf16[16,16,128]{2,1,0:T(8,128)(2,1)S(1)} %collective-permute-done.8) | copy-start | bytes 196612
  68.1 5.3 copy-start.30
  68.8 14.2 %collective-permute-start.10 = (bf16[48,16,128]{2,1,0:T(8,128)(2,1)}, bf16[48,16,128]{2,1,0:T(8,128)(2,1)}, u32[]{:S(2)}, u32[]{:S(2)}) collective-permute-start(bf16[48,16,128]{2,1,0:T(8,128)(2,1)} %pad_maximum_fusion.1), channel_id=1, source_target_pairs={{0,8},{8,16},{16,24},{24,32},{32,40},{40,48},{48,56},{56,64},{64,7... | collective-permute-start | bytes 589832 | tf_op jit(solution)/shard_map/ppermute | solution.py:23
  71.4 11.5 %collective-permute-start.11 = (bf16[48,16,128]{2,1,0:T(8,128)(2,1)}, bf16[48,16,128]{2,1,0:T(8,128)(2,1)}, u32[]{:S(2)}, u32[]{:S(2)}) collective-permute-start(bf16[48,16,128]{2,1,0:T(8,128)(2,1)} %pad_maximum_fusion.1), channel_id=1, source_target_pairs={{8,0},{16,8},{24,16},{32,24},{40,32},{48,40},{56,48},{64,56},{72,6... | collective-permute-start | bytes 589832 | tf_op jit(solution)/shard_map/ppermute | solution.py:24
  73.0 1.0 copy-start.1
  75.9 3.8 copy-start
  76.5 3.7 copy-start.13
  78.4 2.1 copy-start.7
  78.8 1.9 copy-start.9
  79.2 1.7 copy-start.11
  79.6 1.5 copy-start.32
  80.7 1.0 copy-start.5
  82.5 0.8 copy-start.29
  82.5 0.9 copy-start.31
  90.1 0.8 copy-start.33
  90.1 1.7 copy-start.12
  90.1 2.5 copy-start.10
  90.1 2.7 copy-start.8
  91.0 6.0 copy-start.14
  102.0 22.5 %copy-start.34 = (bf16[256,128]{1,0:T(8,128)(2,1)S(1)}, bf16[256,128]{1,0:T(8,128)(2,1)}, u32[]{:S(2)}) copy-start(bf16[256,128]{1,0:T(8,128)(2,1)} %convolution_convert_fusion.19) | copy-start | bytes 196612
  141.2 1.0 copy-start.2
  141.2 1.0 copy-start.3
  141.2 1.1 copy-start.4
  146.0 0.8 copy-start.24
  146.0 0.9 copy-start.25
  146.1 0.9 copy-start.26
  146.1 0.9 copy-start.27
  146.1 1.7 copy-start.16
  146.1 1.7 copy-start.17
  146.1 1.7 copy-start.18
  146.1 1.7 copy-start.19
  146.1 1.7 copy-start.20
  146.1 1.7 copy-start.21
  146.1 1.7 copy-start.22
  146.1 1.7 copy-start.23
  149.9 772.6 %all-reduce.47.cloned.1.call-start = ((), (), s32[]{:S(2)}) async-start(), calls=%async_computation | async-start | bytes 4587520 | tf_op jit(solution)/shard_map/psum | solution.py:171
  378.1 21.4 %collective-permute-start.4 = (bf16[16,48,128]{2,1,0:T(8,128)(2,1)S(1)}, bf16[16,48,128]{2,1,0:T(8,128)(2,1)S(1)}, u32[]{:S(2)}, u32[]{:S(2)}) collective-permute-start(bf16[16,48,128]{2,1,0:T(8,128)(2,1)S(1)} %get-tuple-element.113), channel_id=1, source_target_pairs={{0,1},{1,2},{2,3},{3,4},{4,5},{5,6},{6,7},{8,9},{9,10},{10,11},{11... | collective-permute-start | bytes 589832 | tf_op jit(solution)/shard_map/ppermute | solution.py:13
  382.7 17.9 %collective-permute-start.5 = (bf16[16,48,128]{2,1,0:T(8,128)(2,1)S(1)}, bf16[16,48,128]{2,1,0:T(8,128)(2,1)S(1)}, u32[]{:S(2)}, u32[]{:S(2)}) collective-permute-start(bf16[16,48,128]{2,1,0:T(8,128)(2,1)S(1)} %get-tuple-element.114), channel_id=1, source_target_pairs={{1,0},{2,1},{3,2},{4,3},{5,4},{6,5},{7,6},{9,8},{10,9},{11,10},{12... | collective-permute-start | bytes 589832 | tf_op jit(solution)/shard_map/ppermute | solution.py:13
  388.8 23.1 %collective-permute-start.12 = (bf16[16,48,128]{2,1,0:T(8,128)(2,1)S(1)}, bf16[16,48,128]{2,1,0:T(8,128)(2,1)S(1)}, u32[]{:S(2)}, u32[]{:S(2)}) collective-permute-start(bf16[16,48,128]{2,1,0:T(8,128)(2,1)S(1)} %get-tuple-element.111), channel_id=1, source_target_pairs={{0,1},{1,2},{2,3},{3,4},{4,5},{5,6},{6,7},{8,9},{9,10},{10,11},{11... | collective-permute-start | bytes 589832 | tf_op jit(solution)/shard_map/ppermute | solution.py:13
  392.5 21.5 %collective-permute-start.13 = (bf16[16,48,128]{2,1,0:T(8,128)(2,1)S(1)}, bf16[16,48,128]{2,1,0:T(8,128)(2,1)S(1)}, u32[]{:S(2)}, u32[]{:S(2)}) collective-permute-start(bf16[16,48,128]{2,1,0:T(8,128)(2,1)S(1)} %get-tuple-element.112), channel_id=1, source_target_pairs={{1,0},{2,1},{3,2},{4,3},{5,4},{6,5},{7,6},{9,8},{10,9},{11,10},{12... | collective-permute-start | bytes 589832 | tf_op jit(solution)/shard_map/ppermute | solution.py:13
  400.7 16.0 %collective-permute-start.6 = (bf16[16,16,128]{2,1,0:T(8,128)(2,1)S(1)}, bf16[16,16,128]{2,1,0:T(8,128)(2,1)S(1)}, u32[]{:S(2)}, u32[]{:S(2)}) collective-permute-start(bf16[16,16,128]{2,1,0:T(8,128)(2,1)S(1)} %get-tuple-element.131), channel_id=1, source_target_pairs={{0,8},{8,16},{16,24},{24,32},{32,40},{40,48},{48,56},{56,64},{64,7... | collective-permute-start | bytes 196616 | tf_op jit(solution)/shard_map/ppermute | solution.py:13
  402.0 14.7 %collective-permute-start.7 = (bf16[16,16,128]{2,1,0:T(8,128)(2,1)S(1)}, bf16[16,16,128]{2,1,0:T(8,128)(2,1)S(1)}, u32[]{:S(2)}, u32[]{:S(2)}) collective-permute-start(bf16[16,16,128]{2,1,0:T(8,128)(2,1)S(1)} %get-tuple-element.132), channel_id=1, source_target_pairs={{8,0},{16,8},{24,16},{32,24},{40,32},{48,40},{56,48},{64,56},{72,6... | collective-permute-start | bytes 196616 | tf_op jit(solution)/shard_map/ppermute | solution.py:13
  414.1 3.4 collective-permute-start.14
  415.5 9.5 %collective-permute-start.15 = (bf16[16,16,128]{2,1,0:T(8,128)(2,1)S(1)}, bf16[16,16,128]{2,1,0:T(8,128)(2,1)S(1)}, u32[]{:S(2)}, u32[]{:S(2)}) collective-permute-start(bf16[16,16,128]{2,1,0:T(8,128)(2,1)S(1)} %get-tuple-element.130), channel_id=1, source_target_pairs={{8,0},{16,8},{24,16},{32,24},{40,32},{48,40},{56,48},{64,56},{72,6... | collective-permute-start | bytes 196616 | tf_op jit(solution)/shard_map/ppermute | solution.py:13
  922.5 2.5 copy-start.6
  925.0 1.3 copy-start.15
Sparse Core Ops, SparseCore 0:
  150.1 222.9 all-reduce.48
  376.2 546.2 all-reduce.46
